TPU v7x, 32 devices: a whole 2x2x4 slice. The times are simulated.
32 devices in a mesh: gx: 4 (over x, core), gy: 8 (over z, y).
Axes of the slice: x: 2, y: 2, z: 4, core: 2. Of those that a mesh axis runs over, the one named last changes fastest.
Arguments:
- thickness: float32 [8, 512, 1024], P(None, 'gy', 'gx'), may hold values from 1 to 2
- velocity: float32 [2, 8, 512, 1024], P(None, None, 'gy', 'gx'), may hold values from -3 to 3
- bottom: float32 [512, 1024], P('gy', 'gx'), may hold values from -2 to 2
- coriolis: float32 [512, 1024], P('gy', 'gx'), may hold values from -4 to 4
- reduced: float32 [8], replicated, may hold values from 0.2 to 2
Outputs:
- thickness_new: float32 [8, 512, 1024], P(None, 'gy', 'gx')
- velocity_new: float32 [2, 8, 512, 1024], P(None, None, 'gy', 'gx')
All inputs are finite; a program needn't handle non-finite values.
Results may differ from a plain program's by a relative error of at most 0.00002.
Values sent between devices are 32-bit elements; how exact they have to be, the bound alone decides.
A program may use at most 128 MiB of HBM per device.

v0:
```python
import jax
import jax.numpy as jnp
from jax import lax
from jax.experimental import pallas as pl
from jax.experimental.pallas import tpu as pltpu
from jax.sharding import PartitionSpec as P

time_step = 0.1
LANES = 128
SUB = 8
GROUP = 16
UNROLL = 10
MESH = pl.DeviceIdType.MESH


def kernel(
    count_x, count_y, rows,
    h_in, vel_in, bottom_in, coriolis_in, reduced_in,
    h_out, vel_out,
    own, mid, result, edge_send, edge_recv, fixed, strip, strip_mid, pack, west_pack, east_pack,
    reduced_local, load_sem, store_sem, small_sem, send_sem, recv_sem,
):
    levels = SUB
    blocks = rows // SUB
    ext = rows + 2 * SUB
    me_x = lax.axis_index("gx")
    me_y = lax.axis_index("gy")
    west_open = me_x > 0
    east_open = me_x < count_x - 1
    north = lax.rem(me_y + 1, count_y)
    south = lax.rem(me_y + count_y - 1, count_y)

    loads = []
    for half in range(2):
        cols = pl.ds(half * LANES, LANES)
        sources = [h_in.at[:, :, cols], vel_in.at[0, :, :, cols], vel_in.at[1, :, :, cols]]
        for item in range(3):
            loads.append(pltpu.make_async_copy(sources[item], own.at[item, half], load_sem.at[half, item]))
        for item, source in enumerate((bottom_in, coriolis_in)):
            loads.append(
                pltpu.make_async_copy(
                    source.at[:, cols], fixed.at[item, half, pl.ds(SUB, rows)], load_sem.at[half, 3 + item]
                )
            )
    loads.append(pltpu.make_async_copy(reduced_in, reduced_local, small_sem))
    for copy in loads:
        copy.start()

    barrier = pltpu.get_barrier_semaphore()

    def greet(x, y):
        pl.semaphore_signal(barrier, inc=1, device_id={"gx": x, "gy": y}, device_id_type=MESH)

    greet(me_x, north)
    greet(me_x, south)

    @pl.when(west_open)
    def _():
        for y in (north, me_y, south):
            greet(me_x - 1, y)

    @pl.when(east_open)
    def _():
        for y in (north, me_y, south):
            greet(me_x + 1, y)

    @pl.when(jnp.logical_not(west_open))
    def _():
        west_pack[...] = jnp.zeros_like(west_pack)

    @pl.when(jnp.logical_not(east_open))
    def _():
        east_pack[...] = jnp.zeros_like(east_pack)

    lane = lax.broadcasted_iota(jnp.int32, (SUB, LANES), 1)
    sub = lax.broadcasted_iota(jnp.int32, (SUB, LANES), 0)
    level = lane // GROUP
    place = lane - level * GROUP
    for copy in loads:
        copy.wait()
    reduced_main = jnp.zeros((SUB, LANES), jnp.float32)
    reduced_strip = jnp.zeros((SUB, LANES), jnp.float32)
    for item in range(levels):
        value = 2.0 * reduced_local[item]
        reduced_main = jnp.where(sub == item, value, reduced_main)
        reduced_strip = jnp.where(level == item, value, reduced_strip)

    def turn(values, shift):
        return pltpu.roll(values, shift % LANES, 1)

    flat = [[own.at[item, half].reshape(levels * rows, LANES) for half in range(2)] for item in range(3)]

    def own_row(item, half, row):
        return flat[item][half][pl.ds(row, levels, stride=rows), :]

    for item in range(3):
        for half in range(2):
            for row in range(2):
                edge_send[0, item, half, row] = own_row(item, half, rows - 2 + row)
                edge_send[1, item, half, row] = own_row(item, half, row)

    wall_last = jnp.logical_and(place == 13, jnp.logical_not(east_open))

    def spread(gathered):
        left = turn(gathered, -6)
        right = turn(gathered, 6)
        return jnp.where(place < 8, left, right)

    def build(block, _):
        base = pl.multiple_of(block * SUB, SUB)
        after = pl.multiple_of(block * SUB + SUB, SUB)
        made = []
        for item in range(3):
            gathered = jnp.zeros((SUB, LANES), jnp.float32)
            for lev in range(levels):
                low = own[item, 0, lev, pl.ds(base, SUB), :]
                high = own[item, 1, lev, pl.ds(base, SUB), :]
                joined = jnp.where(lane < LANES // 2, low, high)
                gathered = jnp.where(level == lev, turn(joined, GROUP * lev + 8), gathered)
            value = spread(gathered)
            if item == 1:
                value = jnp.where(wall_last, 0.0, value)
            made.append(value)
        for item in range(2):
            low = fixed[item, 0, pl.ds(after, SUB), :]
            high = fixed[item, 1, pl.ds(after, SUB), :]
            joined = turn(jnp.where(lane < LANES // 2, low, high), 8)
            gathered = jnp.where(lane < GROUP, joined, 0.0)
            for shift in (16, 32, 64):
                gathered = gathered + turn(gathered, shift)
            made.append(spread(gathered))
        for item in range(5):
            strip[item, pl.ds(after, SUB), :] = made[item]
        eastbound = turn(made[4], -4)
        westbound = turn(made[4], 4)
        for item in (3, 2, 1, 0):
            eastbound = jnp.where(place < 2 * item + 2, turn(made[item], 2 * item - 12), eastbound)
            westbound = jnp.where(place >= 14 - 2 * item, turn(made[item], 12 - 2 * item), westbound)
        pack[0, pl.ds(base, SUB), :] = eastbound
        pack[1, pl.ds(base, SUB), :] = westbound
        return 0

    lax.fori_loop(0, blocks, build, 0)

    first = pl.ds(0, SUB)
    last = pl.ds(rows - SUB, SUB)
    own_first = pl.ds(SUB, SUB)
    own_last = pl.ds(rows, SUB)
    ext_last = pl.ds(rows + SUB, SUB)
    ext_own = pl.ds(SUB, rows)

    def remote(index, source, target, x, y):
        return pltpu.make_async_remote_copy(
            src_ref=source,
            dst_ref=target,
            send_sem=send_sem.at[index],
            recv_sem=recv_sem.at[index],
            device_id={"gx": x, "gy": y},
            device_id_type=MESH,
        )

    along_y = [
        remote(0, edge_send.at[0], edge_recv.at[0], me_x, north),
        remote(1, edge_send.at[1], edge_recv.at[1], me_x, south),
        remote(2, fixed.at[:, :, own_last], fixed.at[:, :, first], me_x, north),
        remote(3, fixed.at[:, :, own_first], fixed.at[:, :, ext_last], me_x, south),
        remote(4, strip.at[:, own_last], strip.at[:, first], me_x, north),
        remote(5, strip.at[:, own_first], strip.at[:, ext_last], me_x, south),
    ]
    to_east = [
        remote(6, pack.at[0], west_pack.at[ext_own], me_x + 1, me_y),
        remote(7, pack.at[0, last], west_pack.at[first], me_x + 1, north),
        remote(8, pack.at[0, first], west_pack.at[ext_last], me_x + 1, south),
    ]
    to_west = [
        remote(9, pack.at[1], east_pack.at[ext_own], me_x - 1, me_y),
        remote(10, pack.at[1, last], east_pack.at[first], me_x - 1, north),
        remote(11, pack.at[1, first], east_pack.at[ext_last], me_x - 1, south),
    ]

    greeted = 2 + 3 * west_open.astype(jnp.int32) + 3 * east_open.astype(jnp.int32)
    pl.semaphore_wait(barrier, greeted)
    for copy in along_y:
        copy.start()

    @pl.when(east_open)
    def _():
        for copy in to_east:
            copy.start()

    @pl.when(west_open)
    def _():
        for copy in to_west:
            copy.start()

    before_end = lane < LANES - 1
    at_start = lane == 0

    def eastward(pair):
        low, high = turn(pair[0], -1), turn(pair[1], -1)
        return [jnp.where(before_end, low, high), high]

    def westward(pair):
        low, high = turn(pair[0], 1), turn(pair[1], 1)
        return [low, jnp.where(at_start, low, high)]

    def each(function, *pairs):
        return [function(*items) for items in zip(*pairs)]

    def begin(row):
        thick, along_x, along_y = row
        wide = each(lambda a, b: a + b, thick, eastward(thick))
        flux = each(lambda a, b: a * b, wide, along_x)
        zero = [jnp.zeros((SUB, LANES), jnp.float32)] * 2
        return [thick, along_x, along_y, wide, flux, zero, zero, zero]

    def advance(carry, following, bottom_next, coriolis):
        thick, along_x, along_y, wide, flux, bern, flux_y_before, turn_before = carry
        thick_n, along_x_n, along_y_n = following
        wide_n = each(lambda a, b: a + b, thick_n, eastward(thick_n))
        flux_n = each(lambda a, b: a * b, wide_n, along_x_n)
        flux_y = each(lambda a, b, c: (a + b) * c, thick, thick_n, along_y)
        vort = each(
            lambda e, v, un, u, f: (e - v) - (un - u) + f,
            eastward(along_y), along_y, along_x_n, along_x, coriolis,
        )
        spin = each(lambda z, a, b: z / (a + b), vort, wide, wide_n)
        turn_y = each(lambda w, a, b: w * (a + b), spin, flux_y, eastward(flux_y))
        turn_x = each(lambda w, a, b: w * (a + b), spin, flux, flux_n)
        square = each(lambda a: a * a, along_x_n)
        bern_n = each(
            lambda s, w, vn, v, b, h: 0.5 * ((s + w) + (vn * vn + v * v))
            + (b + jnp.sum(h, axis=0, keepdims=True))
            + reduced_main * h,
            square, westward(square), along_y_n, along_y, bottom_next, thick_n,
        )
        rate_h = each(
            lambda f, w, g, p: -((f - w) + (g - p)), flux, westward(flux), flux_y, flux_y_before
        )
        rate_u = each(lambda p, t, e, b: (p + t) - (e - b), turn_before, turn_y, eastward(bern), bern)
        rate_v = each(lambda w, t, n, b: -(w + t) - (n - b), westward(turn_x), turn_x, bern_n, bern)
        carry = [thick_n, along_x_n, along_y_n, wide_n, flux_n, bern_n, flux_y, turn_y]
        return carry, [rate_h, rate_u, rate_v]

    def fixed_row(item, row):
        return [
            jnp.broadcast_to(fixed[item, half, pl.ds(row + SUB, 1), :], (SUB, LANES)) for half in range(2)
        ]

    def start_row(row):
        return [[own_row(item, half, row) for half in range(2)] for item in range(3)]

    def halo_row(side, row):
        return [[edge_recv[side, item, half, row] for half in range(2)] for item in range(3)]

    def mid_row(row):
        return [[mid[item, half, row + 1] for half in range(2)] for item in range(3)]

    def keep_mid(row, carry, rates):
        for item in range(3):
            for half in range(2):
                mid[item, half, row + 1] = carry[item][half] + 0.5 * time_step * rates[item][half]

    def first_step(carry, row, following):
        after, rates = advance(carry, following, fixed_row(0, row + 1), fixed_row(1, row))
        keep_mid(row, carry, rates)
        return after

    def sweep(carry, start, stop, step):
        whole = (stop - start) // UNROLL

        def some(block, carry):
            for extra in range(UNROLL):
                carry = step(carry, start + block * UNROLL + extra)
            return carry

        carry = lax.fori_loop(0, whole, some, carry)
        for row in range(start + whole * UNROLL, stop):
            carry = step(carry, row)
        return carry

    carry = begin(start_row(0))
    carry, _ = advance(carry, start_row(1), fixed_row(0, 1), fixed_row(1, 0))
    sweep(carry, 1, rows - 1, lambda carry, row: first_step(carry, row, start_row(row + 1)))

    out_flat = [[result.at[item, half].reshape(levels * rows, LANES) for half in range(2)] for item in range(3)]

    def second_step(carry, row):
        after, rates = advance(carry, mid_row(row + 1), fixed_row(0, row + 1), fixed_row(1, row))
        start = start_row(row)
        for item in range(3):
            for half in range(2):
                value = 0.5 * (start[item][half] + carry[item][half]) + 0.25 * time_step * rates[item][half]
                out_flat[item][half][pl.ds(row, levels, stride=rows), :] = value
        return after

    def second_sweep(start, stop):
        carry = begin(mid_row(start - 1))
        carry, _ = advance(carry, mid_row(start), fixed_row(0, start), fixed_row(1, start - 1))
        sweep(carry, start, stop, second_step)

    second_sweep(2, rows - 2)

    for copy in along_y[:4]:
        copy.wait_recv()
    south_rows = [halo_row(0, 0), halo_row(0, 1), start_row(0), start_row(1)]
    carry = begin(south_rows[0])
    carry, _ = advance(carry, south_rows[1], fixed_row(0, -1), fixed_row(1, -2))
    for row in (-1, 0):
        carry = first_step(carry, row, south_rows[row + 3])
    north_rows = [start_row(rows - 2), start_row(rows - 1), halo_row(1, 0), halo_row(1, 1)]
    carry = begin(north_rows[0])
    carry, _ = advance(carry, north_rows[1], fixed_row(0, rows - 1), fixed_row(1, rows - 2))
    for step in range(2):
        carry = first_step(carry, rows - 1 + step, north_rows[step + 2])
    second_sweep(0, 2)
    second_sweep(rows - 2, rows)

    for copy in along_y[4:]:
        copy.wait_recv()

    @pl.when(west_open)
    def _():
        for copy in to_east:
            copy.wait_recv()

    @pl.when(east_open)
    def _():
        for copy in to_west:
            copy.wait_recv()

    wide_lane = lax.broadcasted_iota(jnp.int32, (ext, LANES), 1)
    wide_place = wide_lane - (wide_lane // GROUP) * GROUP
    from_west = wide_place < 2
    from_east = wide_place >= 14
    outside = jnp.logical_or(
        jnp.logical_and(from_west, jnp.logical_not(west_open)),
        jnp.logical_and(from_east, jnp.logical_not(east_open)),
    )
    closed = jnp.logical_or(outside, jnp.logical_and(wide_place == 13, jnp.logical_not(east_open)))
    received_west = west_pack[...]
    received_east = east_pack[...]
    fields = []
    for item in range(5):
        value = jnp.where(from_west, turn(received_west, -2 * item), strip[item])
        fields.append(jnp.where(from_east, turn(received_east, 2 * item), value))
    weight = jnp.concatenate([reduced_strip] * (ext // SUB), axis=0)

    def strip_rates(thick, along_x, along_y, bottom, coriolis):
        def north_of(values):
            return pltpu.roll(values, ext - 1, 0)

        def south_of(values):
            return pltpu.roll(values, 1, 0)

        wide = thick + turn(thick, -1)
        flux = wide * along_x
        flux_y = (thick + north_of(thick)) * along_y
        vort = (turn(along_y, -1) - along_y) - (north_of(along_x) - along_x) + coriolis
        spin = vort / (wide + north_of(wide))
        turn_y = spin * (flux_y + turn(flux_y, -1))
        turn_x = spin * (flux + north_of(flux))
        square = along_x * along_x
        square_y = along_y * along_y
        total = thick
        for shift in (16, 32, 64):
            total = total + turn(total, shift)
        bern = 0.5 * ((square + turn(square, 1)) + (square_y + south_of(square_y))) + (bottom + total) + weight * thick
        rate_h = -((flux - turn(flux, 1)) + (flux_y - south_of(flux_y)))
        rate_u = (south_of(turn_y) + turn_y) - (turn(bern, -1) - bern)
        rate_v = -(turn(turn_x, 1) + turn_x) - (north_of(bern) - bern)
        return rate_h, rate_u, rate_v

    rates = strip_rates(*fields)
    middle = []
    for item in range(3):
        value = fields[item] + 0.5 * time_step * rates[item]
        middle.append(jnp.where(closed if item == 1 else outside, 0.0, value))
    rates = strip_rates(*middle, fields[3], fields[4])
    for item in range(3):
        value = 0.5 * (fields[item] + middle[item]) + 0.25 * time_step * rates[item]
        if item == 1:
            value = jnp.where(closed, 0.0, value)
        strip_mid[item] = jnp.where(wide_place < 8, turn(value, -6), turn(value, 6))

    def merge(block, _):
        base = pl.multiple_of(block * SUB, SUB)
        after = pl.multiple_of(block * SUB + SUB, SUB)
        for item in range(3):
            value = strip_mid[item, pl.ds(after, SUB), :]
            for lev in range(levels):
                moved = turn(value, -(GROUP * lev + 8))
                low = result[item, 0, lev, pl.ds(base, SUB), :]
                high = result[item, 1, lev, pl.ds(base, SUB), :]
                result[item, 0, lev, pl.ds(base, SUB), :] = jnp.where(lane < 2, moved, low)
                result[item, 1, lev, pl.ds(base, SUB), :] = jnp.where(lane >= LANES - 4, moved, high)
        return 0

    stores = []
    half_blocks = (blocks + 1) // 2
    for group, (start, stop) in enumerate(((0, half_blocks), (half_blocks, blocks))):
        lax.fori_loop(start, stop, merge, 0)
        part = pl.ds(start * SUB, (stop - start) * SUB)
        for half in range(2):
            cols = pl.ds(half * LANES, LANES)
            targets = [h_out.at[:, part, cols], vel_out.at[0, :, part, cols], vel_out.at[1, :, part, cols]]
            for item in range(3):
                copy = pltpu.make_async_copy(
                    result.at[item, half, :, part], targets[item], store_sem.at[group, half, item]
                )
                copy.start()
                stores.append(copy)
    for copy in along_y:
        copy.wait_send()

    @pl.when(east_open)
    def _():
        for copy in to_east:
            copy.wait_send()

    @pl.when(west_open)
    def _():
        for copy in to_west:
            copy.wait_send()

    for copy in stores:
        copy.wait()


def solution(mesh):
    count_x, count_y = mesh.shape["gx"], mesh.shape["gy"]

    def body(thickness, velocity, bottom, coriolis, reduced):
        levels, rows, columns = thickness.shape
        assert levels == SUB and columns == 2 * LANES and rows % SUB == 0
        ext = rows + 2 * SUB
        f32 = jnp.float32

        def run(*refs):
            kernel(count_x, count_y, rows, *refs)

        in_hbm = pl.BlockSpec(memory_space=pltpu.HBM)
        return pl.pallas_call(
            run,
            out_shape=(
                jax.ShapeDtypeStruct(thickness.shape, f32),
                jax.ShapeDtypeStruct(velocity.shape, f32),
            ),
            in_specs=[in_hbm] * 5,
            out_specs=(in_hbm, in_hbm),
            scratch_shapes=[
                pltpu.VMEM((3, 2, levels, rows, LANES), f32),
                pltpu.VMEM((3, 2, rows + 2, levels, LANES), f32),
                pltpu.VMEM((3, 2, levels, rows, LANES), f32),
                pltpu.VMEM((2, 3, 2, 2, levels, LANES), f32),
                pltpu.VMEM((2, 3, 2, 2, levels, LANES), f32),
                pltpu.VMEM((2, 2, ext, LANES), f32),
                pltpu.VMEM((5, ext, LANES), f32),
                pltpu.VMEM((3, ext, LANES), f32),
                pltpu.VMEM((2, rows, LANES), f32),
                pltpu.VMEM((ext, LANES), f32),
                pltpu.VMEM((ext, LANES), f32),
                pltpu.SMEM((levels,), f32),
                pltpu.SemaphoreType.DMA((2, 5)),
                pltpu.SemaphoreType.DMA((2, 2, 3)),
                pltpu.SemaphoreType.DMA,
                pltpu.SemaphoreType.DMA((12,)),
                pltpu.SemaphoreType.DMA((12,)),
            ],
            compiler_params=pltpu.CompilerParams(
                collective_id=0, has_side_effects=True, vmem_limit_bytes=62 * 1024 * 1024
            ),
            cost_estimate=pl.CostEstimate(
                flops=200 * thickness.size, bytes_accessed=28 * thickness.size, transcendentals=0
            ),
        )(thickness, velocity, bottom, coriolis, reduced)

    return jax.shard_map(
        body,
        mesh=mesh,
        in_specs=(P(None, "gy", "gx"), P(None, None, "gy", "gx"), P("gy", "gx"), P("gy", "gx"), P()),
        out_specs=(P(None, "gy", "gx"), P(None, None, "gy", "gx")),
        check_vma=False,
    )
```

profile of v0, /device:TPU:1, one launch (start us, length us, event | category | flops | bytes accessed | tf_op | source)
XLA Modules:
  0.0 20.1 jit_solution(3747554855947731644)
XLA Ops:
  0.6 16.6 %shard_map.68 = (f32[8,64,256]{2,1,0:T(8,128)}, f32[2,8,64,256]{3,2,1,0:T(8,128)}) custom-call(f32[8,64,256]{2,1,0:T(8,128)} %refs_0_.1, f32[2,8,64,256]{3,2,1,0:T(8,128)} %refs_1_.1, f32[64,256]{1,0:T(8,128)} %refs_2_.1, f32[64,256]{1,0:T(8,128)} %refs_3_.1, f32[8]{0:T(128)} %refs_4_.1), custom_call_target="tpu_custom_call" | custom-call | flops 26214400 | bytes 3670016 | tf_op jit(solution)/shard_map/pallas_call | solution.py:443
  17.2 0.0 copy-start
  17.2 2.0 %copy.9 = f32[8,64,256]{2,1,0:T(8,128)} copy(f32[8,64,256]{2,1,0:T(8,128)} %get-tuple-element.4) | data formatting | bytes 1048576
  19.2 0.0 copy-done
  19.2 1.0 %copy.10 = f32[2,8,64,256]{3,2,1,0:T(8,128)} copy(f32[2,8,64,256]{3,2,1,0:T(8,128)S(1)} %copy-done) | data formatting | bytes 2097152
Async XLA Ops:
  17.2 2.0 %copy-start = (f32[2,8,64,256]{3,2,1,0:T(8,128)S(1)}, f32[2,8,64,256]{3,2,1,0:T(8,128)}, u32[]{:S(2)}) copy-start(f32[2,8,64,256]{3,2,1,0:T(8,128)} %get-tuple-element.5) | copy-start | bytes 3145732
where the time goes:
time: 20.3 us; the launch traced here: 20.1 us
  Pallas kernels  16.6 us (82%)
  local copies, waits for them, and re-layouts  2.93 us (14%)
  between operations  0.65 us (3%)
    pallas_call x1, Pallas kernels, body(): pl.pallas_call(run, out_shape=(jax.ShapeDtypeStruct(thickness.shape, f32)...  16.6 us
    unnamed x4, local copies, waits for them, and re-layouts  2.93 us

commit v1 on v0

--- a/solution.py
+++ b/solution.py
@@ -10,15 +10,17 @@
 SUB = 8
 GROUP = 16
 UNROLL = 10
+VMEM_MAIN = 58 * 1024 * 1024
+VMEM_END = 16 * 1024 * 1024
 MESH = pl.DeviceIdType.MESH
 
 
 def kernel(
     count_x, count_y, rows,
     h_in, vel_in, bottom_in, coriolis_in, reduced_in,
-    h_out, vel_out,
-    own, mid, result, edge_send, edge_recv, fixed, strip, strip_mid, pack, west_pack, east_pack,
-    reduced_local, load_sem, store_sem, small_sem, send_sem, recv_sem,
+    result, strip_out,
+    own, mid, edge_send, edge_recv, fixed, strip, pack, west_pack, east_pack,
+    reduced_local, load_sem, small_sem, send_sem, recv_sem,
 ):
     levels = SUB
     blocks = rows // SUB
@@ -381,35 +383,8 @@
         value = 0.5 * (fields[item] + middle[item]) + 0.25 * time_step * rates[item]
         if item == 1:
             value = jnp.where(closed, 0.0, value)
-        strip_mid[item] = jnp.where(wide_place < 8, turn(value, -6), turn(value, 6))
-
-    def merge(block, _):
-        base = pl.multiple_of(block * SUB, SUB)
-        after = pl.multiple_of(block * SUB + SUB, SUB)
-        for item in range(3):
-            value = strip_mid[item, pl.ds(after, SUB), :]
-            for lev in range(levels):
-                moved = turn(value, -(GROUP * lev + 8))
-                low = result[item, 0, lev, pl.ds(base, SUB), :]
-                high = result[item, 1, lev, pl.ds(base, SUB), :]
-                result[item, 0, lev, pl.ds(base, SUB), :] = jnp.where(lane < 2, moved, low)
-                result[item, 1, lev, pl.ds(base, SUB), :] = jnp.where(lane >= LANES - 4, moved, high)
-        return 0
-
-    stores = []
-    half_blocks = (blocks + 1) // 2
-    for group, (start, stop) in enumerate(((0, half_blocks), (half_blocks, blocks))):
-        lax.fori_loop(start, stop, merge, 0)
-        part = pl.ds(start * SUB, (stop - start) * SUB)
-        for half in range(2):
-            cols = pl.ds(half * LANES, LANES)
-            targets = [h_out.at[:, part, cols], vel_out.at[0, :, part, cols], vel_out.at[1, :, part, cols]]
-            for item in range(3):
-                copy = pltpu.make_async_copy(
-                    result.at[item, half, :, part], targets[item], store_sem.at[group, half, item]
-                )
-                copy.start()
-                stores.append(copy)
+        strip_out[item] = jnp.where(wide_place < 8, turn(value, -6), turn(value, 6))
+
     for copy in along_y:
         copy.wait_send()
 
@@ -423,6 +398,28 @@
         for copy in to_west:
             copy.wait_send()
 
+
+def finish(rows, result, strip_out, h_out, vel_out, merged, store_sem):
+    levels = SUB
+    blocks = rows // SUB
+    lane = lax.broadcasted_iota(jnp.int32, (SUB, LANES), 1)
+
+    stores = []
+    for block in range(blocks):
+        part = pl.ds(block * SUB, SUB)
+        for item in range(3):
+            value = strip_out[item, pl.ds(block * SUB + SUB, SUB), :]
+            for lev in range(levels):
+                moved = pltpu.roll(value, LANES - (GROUP * lev + 8) % LANES, 1)
+                low = result[item, 0, lev, part, :]
+                high = result[item, 1, lev, part, :]
+                merged[item, lev, part, pl.ds(0, LANES)] = jnp.where(lane < 2, moved, low)
+                merged[item, lev, part, pl.ds(LANES, LANES)] = jnp.where(lane >= LANES - 4, moved, high)
+        targets = [h_out.at[:, part], vel_out.at[0, :, part], vel_out.at[1, :, part]]
+        for item in range(3):
+            copy = pltpu.make_async_copy(merged.at[item, :, part], targets[item], store_sem.at[block, item])
+            copy.start()
+            stores.append(copy)
     for copy in stores:
         copy.wait()
 
@@ -440,40 +437,59 @@
             kernel(count_x, count_y, rows, *refs)
 
         in_hbm = pl.BlockSpec(memory_space=pltpu.HBM)
-        return pl.pallas_call(
+        in_vmem = pl.BlockSpec(memory_space=pltpu.VMEM)
+        result, strip_out = pl.pallas_call(
             run,
             out_shape=(
-                jax.ShapeDtypeStruct(thickness.shape, f32),
-                jax.ShapeDtypeStruct(velocity.shape, f32),
+                pltpu.VMEM((3, 2, levels, rows, LANES), f32),
+                pltpu.VMEM((3, ext, LANES), f32),
             ),
             in_specs=[in_hbm] * 5,
-            out_specs=(in_hbm, in_hbm),
+            out_specs=(in_vmem, in_vmem),
             scratch_shapes=[
                 pltpu.VMEM((3, 2, levels, rows, LANES), f32),
                 pltpu.VMEM((3, 2, rows + 2, levels, LANES), f32),
-                pltpu.VMEM((3, 2, levels, rows, LANES), f32),
                 pltpu.VMEM((2, 3, 2, 2, levels, LANES), f32),
                 pltpu.VMEM((2, 3, 2, 2, levels, LANES), f32),
                 pltpu.VMEM((2, 2, ext, LANES), f32),
                 pltpu.VMEM((5, ext, LANES), f32),
-                pltpu.VMEM((3, ext, LANES), f32),
                 pltpu.VMEM((2, rows, LANES), f32),
                 pltpu.VMEM((ext, LANES), f32),
                 pltpu.VMEM((ext, LANES), f32),
                 pltpu.SMEM((levels,), f32),
                 pltpu.SemaphoreType.DMA((2, 5)),
-                pltpu.SemaphoreType.DMA((2, 2, 3)),
                 pltpu.SemaphoreType.DMA,
                 pltpu.SemaphoreType.DMA((12,)),
                 pltpu.SemaphoreType.DMA((12,)),
             ],
             compiler_params=pltpu.CompilerParams(
-                collective_id=0, has_side_effects=True, vmem_limit_bytes=62 * 1024 * 1024
+                collective_id=0, has_side_effects=True, vmem_limit_bytes=VMEM_MAIN
             ),
             cost_estimate=pl.CostEstimate(
                 flops=200 * thickness.size, bytes_accessed=28 * thickness.size, transcendentals=0
             ),
         )(thickness, velocity, bottom, coriolis, reduced)
+
+        def end(*refs):
+            finish(rows, *refs)
+
+        return pl.pallas_call(
+            end,
+            out_shape=(
+                jax.ShapeDtypeStruct(thickness.shape, f32),
+                jax.ShapeDtypeStruct(velocity.shape, f32),
+            ),
+            in_specs=[in_vmem] * 2,
+            out_specs=(in_hbm, in_hbm),
+            scratch_shapes=[
+                pltpu.VMEM((3, levels, rows, columns), f32),
+                pltpu.SemaphoreType.DMA((rows // SUB, 3)),
+            ],
+            compiler_params=pltpu.CompilerParams(vmem_limit_bytes=VMEM_END),
+            cost_estimate=pl.CostEstimate(
+                flops=thickness.size, bytes_accessed=24 * thickness.size, transcendentals=0
+            ),
+        )(result, strip_out)
 
     return jax.shard_map(
         body,

time: 20.3 us -> 17 us (0.84)
  local copies, waits for them, and re-layouts: 2.93 us -> 0 us
  Pallas kernels: 16.6 us -> 16.2 us
    unnamed x4 -> x0, local copies, waits for them, and re-layouts: 2.93 us -> none
    pallas_call x1 -> x2, Pallas kernels: 16.6 us -> 16.2 us  [the longest x1 14.8 us: body(): pl.pallas_call(run, out_shape=(pltpu.VMEM((3, 2, levels, rows, LANES), f3...]
where the time goes in v1:
time: 17 us; the launch traced here: 16.8 us
  Pallas kernels  16.2 us (95%)
  between operations  0.64 us (4%)
    pallas_call x1, Pallas kernels, body(): pl.pallas_call(run, out_shape=(pltpu.VMEM((3, 2, levels, rows, LANES), f3...  14.8 us
    pallas_call x1, Pallas kernels, body(): pl.pallas_call(end, out_shape=(jax.ShapeDtypeStruct(thickness.shape, f32)...  1.42 us

profile of v1, /device:TPU:1, one launch (start us, length us, event | category | flops | bytes accessed | tf_op | source)
XLA Modules:
  0.0 16.8 jit_solution(3310954341887214207)
XLA Ops:
  0.6 14.8 %shard_map.68 = (f32[3,2,8,64,128]{4,3,2,1,0:T(8,128)S(1)}, f32[3,80,128]{2,1,0:T(8,128)S(1)}) custom-call(f32[8,64,256]{2,1,0:T(8,128)} %refs_0_.1, f32[2,8,64,256]{3,2,1,0:T(8,128)} %refs_1_.1, f32[64,256]{1,0:T(8,128)} %refs_2_.1, f32[64,256]{1,0:T(8,128)} %refs_3_.1, f32[8]{0:T(128)} %refs_4_.1), custom_call_target="tpu_custom_call" | custom-call | flops 26214400 | bytes 3670016 | tf_op jit(solution)/shard_map/pallas_call | solution.py:441
  15.4 1.4 %shard_map.69 = (f32[8,64,256]{2,1,0:T(8,128)}, f32[2,8,64,256]{3,2,1,0:T(8,128)}) custom-call(f32[3,2,8,64,128]{4,3,2,1,0:T(8,128)S(1)} %get-tuple-element.4.refs_0_, f32[3,80,128]{2,1,0:T(8,128)S(1)} %get-tuple-element.5.refs_1_), custom_call_target="tpu_custom_call" | custom-call | flops 131072 | bytes 3145728 | tf_op jit(solution)/shard_map/pallas_call | solution.py:476

commit v2 on v1

--- a/solution.py
+++ b/solution.py
@@ -10,6 +10,7 @@
 SUB = 8
 GROUP = 16
 UNROLL = 10
+GROUPS = 2
 VMEM_MAIN = 58 * 1024 * 1024
 VMEM_END = 16 * 1024 * 1024
 MESH = pl.DeviceIdType.MESH
@@ -19,8 +20,8 @@
     count_x, count_y, rows,
     h_in, vel_in, bottom_in, coriolis_in, reduced_in,
     result, strip_out,
-    own, mid, edge_send, edge_recv, fixed, strip, pack, west_pack, east_pack,
-    reduced_local, load_sem, small_sem, send_sem, recv_sem,
+    own, by_row, mid, fixed, strip, pack, west_pack, east_pack,
+    reduced_local, load_sem, small_sem, row_sem, send_sem, recv_sem,
 ):
     levels = SUB
     blocks = rows // SUB
@@ -45,7 +46,14 @@
                 )
             )
     loads.append(pltpu.make_async_copy(reduced_in, reduced_local, small_sem))
-    for copy in loads:
+    row_loads = []
+    for item in range(3):
+        for lev in range(levels):
+            source = h_in.at[lev] if item == 0 else vel_in.at[item - 1, lev]
+            row_loads.append(
+                pltpu.make_async_copy(source, by_row.at[item, pl.ds(2, rows), lev], row_sem.at[item, lev])
+            )
+    for copy in loads + row_loads:
         copy.start()
 
     barrier = pltpu.get_barrier_semaphore()
@@ -76,8 +84,8 @@
 
     lane = lax.broadcasted_iota(jnp.int32, (SUB, LANES), 1)
     sub = lax.broadcasted_iota(jnp.int32, (SUB, LANES), 0)
-    level = lane // GROUP
-    place = lane - level * GROUP
+    level = levels - 1 - lane // GROUP
+    place = lane % GROUP
     for copy in loads:
         copy.wait()
     reduced_main = jnp.zeros((SUB, LANES), jnp.float32)
@@ -89,17 +97,6 @@
 
     def turn(values, shift):
         return pltpu.roll(values, shift % LANES, 1)
-
-    flat = [[own.at[item, half].reshape(levels * rows, LANES) for half in range(2)] for item in range(3)]
-
-    def own_row(item, half, row):
-        return flat[item][half][pl.ds(row, levels, stride=rows), :]
-
-    for item in range(3):
-        for half in range(2):
-            for row in range(2):
-                edge_send[0, item, half, row] = own_row(item, half, rows - 2 + row)
-                edge_send[1, item, half, row] = own_row(item, half, row)
 
     wall_last = jnp.logical_and(place == 13, jnp.logical_not(east_open))
 
@@ -118,7 +115,7 @@
                 low = own[item, 0, lev, pl.ds(base, SUB), :]
                 high = own[item, 1, lev, pl.ds(base, SUB), :]
                 joined = jnp.where(lane < LANES // 2, low, high)
-                gathered = jnp.where(level == lev, turn(joined, GROUP * lev + 8), gathered)
+                gathered = jnp.where(level == lev, turn(joined, GROUP * (levels - 1 - lev) + 8), gathered)
             value = spread(gathered)
             if item == 1:
                 value = jnp.where(wall_last, 0.0, value)
@@ -142,7 +139,9 @@
         pack[1, pl.ds(base, SUB), :] = westbound
         return 0
 
-    lax.fori_loop(0, blocks, build, 0)
+    lax.fori_loop(0, blocks, build, 0, unroll=4)
+    for copy in row_loads:
+        copy.wait()
 
     first = pl.ds(0, SUB)
     last = pl.ds(rows - SUB, SUB)
@@ -162,8 +161,8 @@
         )
 
     along_y = [
-        remote(0, edge_send.at[0], edge_recv.at[0], me_x, north),
-        remote(1, edge_send.at[1], edge_recv.at[1], me_x, south),
+        remote(0, by_row.at[:, pl.ds(rows, 2)], by_row.at[:, pl.ds(0, 2)], me_x, north),
+        remote(1, by_row.at[:, pl.ds(2, 2)], by_row.at[:, pl.ds(rows + 2, 2)], me_x, south),
         remote(2, fixed.at[:, :, own_last], fixed.at[:, :, first], me_x, north),
         remote(3, fixed.at[:, :, own_first], fixed.at[:, :, ext_last], me_x, south),
         remote(4, strip.at[:, own_last], strip.at[:, first], me_x, north),
@@ -249,22 +248,23 @@
             jnp.broadcast_to(fixed[item, half, pl.ds(row + SUB, 1), :], (SUB, LANES)) for half in range(2)
         ]
 
+    def halves(ref, item, row):
+        return [ref[item, row, :, pl.ds(half * LANES, LANES)] for half in range(2)]
+
     def start_row(row):
-        return [[own_row(item, half, row) for half in range(2)] for item in range(3)]
-
-    def halo_row(side, row):
-        return [[edge_recv[side, item, half, row] for half in range(2)] for item in range(3)]
+        return [halves(by_row, item, row + 2) for item in range(3)]
 
     def mid_row(row):
-        return [[mid[item, half, row + 1] for half in range(2)] for item in range(3)]
+        return [halves(mid, item, row + 1) for item in range(3)]
 
     def keep_mid(row, carry, rates):
         for item in range(3):
             for half in range(2):
-                mid[item, half, row + 1] = carry[item][half] + 0.5 * time_step * rates[item][half]
-
-    def first_step(carry, row, following):
-        after, rates = advance(carry, following, fixed_row(0, row + 1), fixed_row(1, row))
+                value = carry[item][half] + 0.5 * time_step * rates[item][half]
+                mid[item, row + 1, :, pl.ds(half * LANES, LANES)] = value
+
+    def first_step(carry, row):
+        after, rates = advance(carry, start_row(row + 1), fixed_row(0, row + 1), fixed_row(1, row))
         keep_mid(row, carry, rates)
         return after
 
@@ -276,16 +276,18 @@
                 carry = step(carry, start + block * UNROLL + extra)
             return carry
 
-        carry = lax.fori_loop(0, whole, some, carry)
+        if whole:
+            carry = lax.fori_loop(0, whole, some, carry)
         for row in range(start + whole * UNROLL, stop):
             carry = step(carry, row)
         return carry
 
-    carry = begin(start_row(0))
-    carry, _ = advance(carry, start_row(1), fixed_row(0, 1), fixed_row(1, 0))
-    sweep(carry, 1, rows - 1, lambda carry, row: first_step(carry, row, start_row(row + 1)))
-
-    out_flat = [[result.at[item, half].reshape(levels * rows, LANES) for half in range(2)] for item in range(3)]
+    def first_sweep(start, stop):
+        carry = begin(start_row(start - 1))
+        carry, _ = advance(carry, start_row(start), fixed_row(0, start), fixed_row(1, start - 1))
+        sweep(carry, start, stop, first_step)
+
+    first_sweep(1, rows - 1)
 
     def second_step(carry, row):
         after, rates = advance(carry, mid_row(row + 1), fixed_row(0, row + 1), fixed_row(1, row))
@@ -293,7 +295,7 @@
         for item in range(3):
             for half in range(2):
                 value = 0.5 * (start[item][half] + carry[item][half]) + 0.25 * time_step * rates[item][half]
-                out_flat[item][half][pl.ds(row, levels, stride=rows), :] = value
+                result[item, row, :, pl.ds(half * LANES, LANES)] = value
         return after
 
     def second_sweep(start, stop):
@@ -303,33 +305,23 @@
 
     second_sweep(2, rows - 2)
 
-    for copy in along_y[:4]:
+    for copy in along_y:
         copy.wait_recv()
-    south_rows = [halo_row(0, 0), halo_row(0, 1), start_row(0), start_row(1)]
-    carry = begin(south_rows[0])
-    carry, _ = advance(carry, south_rows[1], fixed_row(0, -1), fixed_row(1, -2))
-    for row in (-1, 0):
-        carry = first_step(carry, row, south_rows[row + 3])
-    north_rows = [start_row(rows - 2), start_row(rows - 1), halo_row(1, 0), halo_row(1, 1)]
-    carry = begin(north_rows[0])
-    carry, _ = advance(carry, north_rows[1], fixed_row(0, rows - 1), fixed_row(1, rows - 2))
-    for step in range(2):
-        carry = first_step(carry, rows - 1 + step, north_rows[step + 2])
+
+    @pl.when(west_open)
+    def _():
+        for copy in to_east:
+            copy.wait_recv()
+
+    @pl.when(east_open)
+    def _():
+        for copy in to_west:
+            copy.wait_recv()
+
+    first_sweep(-1, 1)
+    first_sweep(rows - 1, rows + 1)
     second_sweep(0, 2)
     second_sweep(rows - 2, rows)
-
-    for copy in along_y[4:]:
-        copy.wait_recv()
-
-    @pl.when(west_open)
-    def _():
-        for copy in to_east:
-            copy.wait_recv()
-
-    @pl.when(east_open)
-    def _():
-        for copy in to_west:
-            copy.wait_recv()
 
     wide_lane = lax.broadcasted_iota(jnp.int32, (ext, LANES), 1)
     wide_place = wide_lane - (wide_lane // GROUP) * GROUP
@@ -401,25 +393,33 @@
 
 def finish(rows, result, strip_out, h_out, vel_out, merged, store_sem):
     levels = SUB
-    blocks = rows // SUB
     lane = lax.broadcasted_iota(jnp.int32, (SUB, LANES), 1)
+    size = rows // GROUPS
 
     stores = []
-    for block in range(blocks):
-        part = pl.ds(block * SUB, SUB)
+    for group in range(GROUPS):
+
+        def merge(step, _):
+            row = group * size + step
+            for item in range(3):
+                value = jnp.broadcast_to(strip_out[item, pl.ds(row + SUB, 1), :], (SUB, LANES))
+                moved = pltpu.roll(value, SUB, 1, stride=GROUP, stride_axis=0)
+                low = result[item, row, :, pl.ds(0, LANES)]
+                high = result[item, row, :, pl.ds(LANES, LANES)]
+                merged[item, row, :, pl.ds(0, LANES)] = jnp.where(lane < 2, moved, low)
+                merged[item, row, :, pl.ds(LANES, LANES)] = jnp.where(lane >= LANES - 4, moved, high)
+            return 0
+
+        lax.fori_loop(0, size, merge, 0, unroll=SUB)
+        part = pl.ds(group * size, size)
         for item in range(3):
-            value = strip_out[item, pl.ds(block * SUB + SUB, SUB), :]
             for lev in range(levels):
-                moved = pltpu.roll(value, LANES - (GROUP * lev + 8) % LANES, 1)
-                low = result[item, 0, lev, part, :]
-                high = result[item, 1, lev, part, :]
-                merged[item, lev, part, pl.ds(0, LANES)] = jnp.where(lane < 2, moved, low)
-                merged[item, lev, part, pl.ds(LANES, LANES)] = jnp.where(lane >= LANES - 4, moved, high)
-        targets = [h_out.at[:, part], vel_out.at[0, :, part], vel_out.at[1, :, part]]
-        for item in range(3):
-            copy = pltpu.make_async_copy(merged.at[item, :, part], targets[item], store_sem.at[block, item])
-            copy.start()
-            stores.append(copy)
+                target = h_out.at[lev, part] if item == 0 else vel_out.at[item - 1, lev, part]
+                copy = pltpu.make_async_copy(
+                    merged.at[item, part, lev], target, store_sem.at[group, item, lev]
+                )
+                copy.start()
+                stores.append(copy)
     for copy in stores:
         copy.wait()
 
@@ -441,16 +441,15 @@
         result, strip_out = pl.pallas_call(
             run,
             out_shape=(
-                pltpu.VMEM((3, 2, levels, rows, LANES), f32),
+                pltpu.VMEM((3, rows, levels, columns), f32),
                 pltpu.VMEM((3, ext, LANES), f32),
             ),
             in_specs=[in_hbm] * 5,
             out_specs=(in_vmem, in_vmem),
             scratch_shapes=[
                 pltpu.VMEM((3, 2, levels, rows, LANES), f32),
-                pltpu.VMEM((3, 2, rows + 2, levels, LANES), f32),
-                pltpu.VMEM((2, 3, 2, 2, levels, LANES), f32),
-                pltpu.VMEM((2, 3, 2, 2, levels, LANES), f32),
+                pltpu.VMEM((3, rows + 4, levels, columns), f32),
+                pltpu.VMEM((3, rows + 2, levels, columns), f32),
                 pltpu.VMEM((2, 2, ext, LANES), f32),
                 pltpu.VMEM((5, ext, LANES), f32),
                 pltpu.VMEM((2, rows, LANES), f32),
@@ -459,6 +458,7 @@
                 pltpu.SMEM((levels,), f32),
                 pltpu.SemaphoreType.DMA((2, 5)),
                 pltpu.SemaphoreType.DMA,
+                pltpu.SemaphoreType.DMA((3, levels)),
                 pltpu.SemaphoreType.DMA((12,)),
                 pltpu.SemaphoreType.DMA((12,)),
             ],
@@ -482,8 +482,8 @@
             in_specs=[in_vmem] * 2,
             out_specs=(in_hbm, in_hbm),
             scratch_shapes=[
-                pltpu.VMEM((3, levels, rows, columns), f32),
-                pltpu.SemaphoreType.DMA((rows // SUB, 3)),
+                pltpu.VMEM((3, rows, levels, columns), f32),
+                pltpu.SemaphoreType.DMA((GROUPS, 3, levels)),
             ],
             compiler_params=pltpu.CompilerParams(vmem_limit_bytes=VMEM_END),
             cost_estimate=pl.CostEstimate(

time: 17 us -> 16 us (0.941)
  Pallas kernels: 16.2 us -> 15.2 us
    pallas_call x1, Pallas kernels: 14.8 us -> 13.1 us  [body(): pl.pallas_call(run, out_shape=(pltpu.VMEM((3, rows, levels, columns), f32...]
    pallas_call x1, Pallas kernels: 1.42 us -> 2.16 us  [body(): pl.pallas_call(end, out_shape=(jax.ShapeDtypeStruct(thickness.shape, f32)...]
where the time goes in v2:
time: 16 us; the launch traced here: 15.9 us
  Pallas kernels  15.2 us (95%)
  between operations  0.64 us (4%)
    pallas_call x1, Pallas kernels, body(): pl.pallas_call(run, out_shape=(pltpu.VMEM((3, rows, levels, columns), f32...  13.1 us
    pallas_call x1, Pallas kernels, body(): pl.pallas_call(end, out_shape=(jax.ShapeDtypeStruct(thickness.shape, f32)...  2.16 us

profile of v2, /device:TPU:1, one launch (start us, length us, event | category | flops | bytes accessed | tf_op | source)
XLA Modules:
  0.0 15.9 jit_solution(1543717568013489559)
XLA Ops:
  0.6 13.1 %shard_map.68 = (f32[3,64,8,256]{3,2,1,0:T(8,128)S(1)}, f32[3,80,128]{2,1,0:T(8,128)S(1)}) custom-call(f32[8,64,256]{2,1,0:T(8,128)} %refs_0_.1, f32[2,8,64,256]{3,2,1,0:T(8,128)} %refs_1_.1, f32[64,256]{1,0:T(8,128)} %refs_2_.1, f32[64,256]{1,0:T(8,128)} %refs_3_.1, f32[8]{0:T(128)} %refs_4_.1), custom_call_target="tpu_custom_call" | custom-call | flops 26214400 | bytes 3670016 | tf_op jit(solution)/shard_map/pallas_call | solution.py:441
  13.7 2.2 %shard_map.69 = (f32[8,64,256]{2,1,0:T(8,128)}, f32[2,8,64,256]{3,2,1,0:T(8,128)}) custom-call(f32[3,64,8,256]{3,2,1,0:T(8,128)S(1)} %get-tuple-element.4.refs_0_, f32[3,80,128]{2,1,0:T(8,128)S(1)} %get-tuple-element.5.refs_1_), custom_call_target="tpu_custom_call" | custom-call | flops 131072 | bytes 3145728 | tf_op jit(solution)/shard_map/pallas_call | solution.py:476

commit v3 on v2

--- a/solution.py
+++ b/solution.py
@@ -10,7 +10,6 @@
 SUB = 8
 GROUP = 16
 UNROLL = 10
-GROUPS = 2
 VMEM_MAIN = 58 * 1024 * 1024
 VMEM_END = 16 * 1024 * 1024
 MESH = pl.DeviceIdType.MESH
@@ -20,8 +19,8 @@
     count_x, count_y, rows,
     h_in, vel_in, bottom_in, coriolis_in, reduced_in,
     result, strip_out,
-    own, by_row, mid, fixed, strip, pack, west_pack, east_pack,
-    reduced_local, load_sem, small_sem, row_sem, send_sem, recv_sem,
+    own, by_row, mid, halo, fixed, strip, pack, west_pack, east_pack,
+    reduced_local, load_sem, fixed_sem, small_sem, row_sem, send_sem, recv_sem,
 ):
     levels = SUB
     blocks = rows // SUB
@@ -39,19 +38,18 @@
         sources = [h_in.at[:, :, cols], vel_in.at[0, :, :, cols], vel_in.at[1, :, :, cols]]
         for item in range(3):
             loads.append(pltpu.make_async_copy(sources[item], own.at[item, half], load_sem.at[half, item]))
-        for item, source in enumerate((bottom_in, coriolis_in)):
-            loads.append(
-                pltpu.make_async_copy(
-                    source.at[:, cols], fixed.at[item, half, pl.ds(SUB, rows)], load_sem.at[half, 3 + item]
-                )
-            )
+    for item, source in enumerate((bottom_in, coriolis_in)):
+        for half in range(2):
+            cols = pl.ds(half * LANES, LANES)
+            target = fixed.at[item, half, pl.ds(SUB, rows)]
+            loads.append(pltpu.make_async_copy(source.at[:, cols], target, fixed_sem.at[item, half]))
     loads.append(pltpu.make_async_copy(reduced_in, reduced_local, small_sem))
     row_loads = []
     for item in range(3):
         for lev in range(levels):
             source = h_in.at[lev] if item == 0 else vel_in.at[item - 1, lev]
             row_loads.append(
-                pltpu.make_async_copy(source, by_row.at[item, pl.ds(2, rows), lev], row_sem.at[item, lev])
+                pltpu.make_async_copy(source, by_row.at[item, :, lev], row_sem.at[item, lev])
             )
     for copy in loads + row_loads:
         copy.start()
@@ -105,17 +103,14 @@
         right = turn(gathered, 6)
         return jnp.where(place < 8, left, right)
 
-    def build(block, _):
-        base = pl.multiple_of(block * SUB, SUB)
-        after = pl.multiple_of(block * SUB + SUB, SUB)
+    def build(read, after):
         made = []
         for item in range(3):
             gathered = jnp.zeros((SUB, LANES), jnp.float32)
             for lev in range(levels):
-                low = own[item, 0, lev, pl.ds(base, SUB), :]
-                high = own[item, 1, lev, pl.ds(base, SUB), :]
-                joined = jnp.where(lane < LANES // 2, low, high)
-                gathered = jnp.where(level == lev, turn(joined, GROUP * (levels - 1 - lev) + 8), gathered)
+                joined = jnp.where(lane < LANES // 2, read(item, 0, lev), read(item, 1, lev))
+                moved = turn(joined, GROUP * (levels - 1 - lev) + 8)
+                gathered = jnp.where(level == lev, moved, gathered)
             value = spread(gathered)
             if item == 1:
                 value = jnp.where(wall_last, 0.0, value)
@@ -130,6 +125,12 @@
             made.append(spread(gathered))
         for item in range(5):
             strip[item, pl.ds(after, SUB), :] = made[item]
+        return made
+
+    def build_own(block, _):
+        base = pl.multiple_of(block * SUB, SUB)
+        after = pl.multiple_of(block * SUB + SUB, SUB)
+        made = build(lambda item, half, lev: own[item, half, lev, pl.ds(base, SUB), :], after)
         eastbound = turn(made[4], -4)
         westbound = turn(made[4], 4)
         for item in (3, 2, 1, 0):
@@ -139,14 +140,12 @@
         pack[1, pl.ds(base, SUB), :] = westbound
         return 0
 
-    lax.fori_loop(0, blocks, build, 0, unroll=4)
+    lax.fori_loop(0, blocks, build_own, 0, unroll=4)
     for copy in row_loads:
         copy.wait()
 
     first = pl.ds(0, SUB)
     last = pl.ds(rows - SUB, SUB)
-    own_first = pl.ds(SUB, SUB)
-    own_last = pl.ds(rows, SUB)
     ext_last = pl.ds(rows + SUB, SUB)
     ext_own = pl.ds(SUB, rows)
 
@@ -160,39 +159,29 @@
             device_id_type=MESH,
         )
 
-    along_y = [
-        remote(0, by_row.at[:, pl.ds(rows, 2)], by_row.at[:, pl.ds(0, 2)], me_x, north),
-        remote(1, by_row.at[:, pl.ds(2, 2)], by_row.at[:, pl.ds(rows + 2, 2)], me_x, south),
-        remote(2, fixed.at[:, :, own_last], fixed.at[:, :, first], me_x, north),
-        remote(3, fixed.at[:, :, own_first], fixed.at[:, :, ext_last], me_x, south),
-        remote(4, strip.at[:, own_last], strip.at[:, first], me_x, north),
-        remote(5, strip.at[:, own_first], strip.at[:, ext_last], me_x, south),
-    ]
+    along_y = []
+    for side, (source_row, row, y) in enumerate(((rows - 2, SUB - 2, north), (0, 0, south))):
+        pair, place_there = pl.ds(source_row, 2), pl.ds(row, 2)
+        copies = []
+        for half in range(2):
+            cols = pl.ds(half * LANES, LANES)
+            copies.append((h_in.at[:, pair, cols], halo.at[side, 0, half, :, place_there]))
+            copies.append((vel_in.at[:, :, pair, cols], halo.at[side, pl.ds(1, 2), half, :, place_there]))
+            outer = pl.ds(row + side * (rows + SUB), 2)
+            copies.append((bottom_in.at[pair, cols], fixed.at[0, half, outer]))
+            copies.append((coriolis_in.at[pair, cols], fixed.at[1, half, outer]))
+        for source, target in copies:
+            along_y.append(remote(6 + len(along_y), source, target, me_x, y))
     to_east = [
-        remote(6, pack.at[0], west_pack.at[ext_own], me_x + 1, me_y),
-        remote(7, pack.at[0, last], west_pack.at[first], me_x + 1, north),
-        remote(8, pack.at[0, first], west_pack.at[ext_last], me_x + 1, south),
+        remote(0, pack.at[0], west_pack.at[ext_own], me_x + 1, me_y),
+        remote(1, pack.at[0, last], west_pack.at[first], me_x + 1, north),
+        remote(2, pack.at[0, first], west_pack.at[ext_last], me_x + 1, south),
     ]
     to_west = [
-        remote(9, pack.at[1], east_pack.at[ext_own], me_x - 1, me_y),
-        remote(10, pack.at[1, last], east_pack.at[first], me_x - 1, north),
-        remote(11, pack.at[1, first], east_pack.at[ext_last], me_x - 1, south),
+        remote(3, pack.at[1], east_pack.at[ext_own], me_x - 1, me_y),
+        remote(4, pack.at[1, last], east_pack.at[first], me_x - 1, north),
+        remote(5, pack.at[1, first], east_pack.at[ext_last], me_x - 1, south),
     ]
-
-    greeted = 2 + 3 * west_open.astype(jnp.int32) + 3 * east_open.astype(jnp.int32)
-    pl.semaphore_wait(barrier, greeted)
-    for copy in along_y:
-        copy.start()
-
-    @pl.when(east_open)
-    def _():
-        for copy in to_east:
-            copy.start()
-
-    @pl.when(west_open)
-    def _():
-        for copy in to_west:
-            copy.start()
 
     before_end = lane < LANES - 1
     at_start = lane == 0
@@ -252,7 +241,16 @@
         return [ref[item, row, :, pl.ds(half * LANES, LANES)] for half in range(2)]
 
     def start_row(row):
-        return [halves(by_row, item, row + 2) for item in range(3)]
+        if isinstance(row, int) and not 0 <= row < rows:
+            side, line = (0, row + SUB) if row < 0 else (1, row - rows)
+            return [
+                [
+                    halo.at[side, item, half].reshape(levels * SUB, LANES)[pl.ds(line, levels, stride=SUB), :]
+                    for half in range(2)
+                ]
+                for item in range(3)
+            ]
+        return [halves(by_row, item, row) for item in range(3)]
 
     def mid_row(row):
         return [halves(mid, item, row + 1) for item in range(3)]
@@ -282,12 +280,33 @@
             carry = step(carry, row)
         return carry
 
-    def first_sweep(start, stop):
+    def first_begin(start):
         carry = begin(start_row(start - 1))
         carry, _ = advance(carry, start_row(start), fixed_row(0, start), fixed_row(1, start - 1))
-        sweep(carry, start, stop, first_step)
-
-    first_sweep(1, rows - 1)
+        return carry
+
+    carry = first_begin(1)
+    early = 1 + UNROLL * ((rows - 2) // (2 * UNROLL))
+    carry = sweep(carry, 1, early, first_step)
+
+    greeted = 2 + 3 * west_open.astype(jnp.int32) + 3 * east_open.astype(jnp.int32)
+    pl.semaphore_wait(barrier, greeted)
+    for copy in along_y:
+        copy.start()
+
+    @pl.when(east_open)
+    def _():
+        for copy in to_east:
+            copy.start()
+
+    @pl.when(west_open)
+    def _():
+        for copy in to_west:
+            copy.start()
+
+    sweep(carry, early, rows - 1, first_step)
+
+    out_flat = [[result.at[item, half].reshape(levels * rows, LANES) for half in range(2)] for item in range(3)]
 
     def second_step(carry, row):
         after, rates = advance(carry, mid_row(row + 1), fixed_row(0, row + 1), fixed_row(1, row))
@@ -295,7 +314,7 @@
         for item in range(3):
             for half in range(2):
                 value = 0.5 * (start[item][half] + carry[item][half]) + 0.25 * time_step * rates[item][half]
-                result[item, row, :, pl.ds(half * LANES, LANES)] = value
+                out_flat[item][half][pl.ds(row, levels, stride=rows), :] = value
         return after
 
     def second_sweep(start, stop):
@@ -318,10 +337,12 @@
         for copy in to_west:
             copy.wait_recv()
 
-    first_sweep(-1, 1)
-    first_sweep(rows - 1, rows + 1)
+    sweep(first_begin(-1), -1, 1, first_step)
+    sweep(first_begin(rows - 1), rows - 1, rows + 1, first_step)
     second_sweep(0, 2)
     second_sweep(rows - 2, rows)
+    for side, after in ((0, 0), (1, rows + SUB)):
+        build(lambda item, half, lev: halo[side, item, half, lev], after)
 
     wide_lane = lax.broadcasted_iota(jnp.int32, (ext, LANES), 1)
     wide_place = wide_lane - (wide_lane // GROUP) * GROUP
@@ -393,33 +414,25 @@
 
 def finish(rows, result, strip_out, h_out, vel_out, merged, store_sem):
     levels = SUB
+    blocks = rows // SUB
     lane = lax.broadcasted_iota(jnp.int32, (SUB, LANES), 1)
-    size = rows // GROUPS
 
     stores = []
-    for group in range(GROUPS):
-
-        def merge(step, _):
-            row = group * size + step
-            for item in range(3):
-                value = jnp.broadcast_to(strip_out[item, pl.ds(row + SUB, 1), :], (SUB, LANES))
-                moved = pltpu.roll(value, SUB, 1, stride=GROUP, stride_axis=0)
-                low = result[item, row, :, pl.ds(0, LANES)]
-                high = result[item, row, :, pl.ds(LANES, LANES)]
-                merged[item, row, :, pl.ds(0, LANES)] = jnp.where(lane < 2, moved, low)
-                merged[item, row, :, pl.ds(LANES, LANES)] = jnp.where(lane >= LANES - 4, moved, high)
-            return 0
-
-        lax.fori_loop(0, size, merge, 0, unroll=SUB)
-        part = pl.ds(group * size, size)
+    for block in range(blocks):
+        part = pl.ds(block * SUB, SUB)
         for item in range(3):
+            value = strip_out[item, pl.ds(block * SUB + SUB, SUB), :]
             for lev in range(levels):
-                target = h_out.at[lev, part] if item == 0 else vel_out.at[item - 1, lev, part]
-                copy = pltpu.make_async_copy(
-                    merged.at[item, part, lev], target, store_sem.at[group, item, lev]
-                )
-                copy.start()
-                stores.append(copy)
+                moved = pltpu.roll(value, (SUB + GROUP * lev) % LANES, 1)
+                low = result[item, 0, lev, part, :]
+                high = result[item, 1, lev, part, :]
+                merged[item, lev, part, pl.ds(0, LANES)] = jnp.where(lane < 2, moved, low)
+                merged[item, lev, part, pl.ds(LANES, LANES)] = jnp.where(lane >= LANES - 4, moved, high)
+        targets = [h_out.at[:, part], vel_out.at[0, :, part], vel_out.at[1, :, part]]
+        for item in range(3):
+            copy = pltpu.make_async_copy(merged.at[item, :, part], targets[item], store_sem.at[block, item])
+            copy.start()
+            stores.append(copy)
     for copy in stores:
         copy.wait()
 
@@ -441,26 +454,28 @@
         result, strip_out = pl.pallas_call(
             run,
             out_shape=(
-                pltpu.VMEM((3, rows, levels, columns), f32),
+                pltpu.VMEM((3, 2, levels, rows, LANES), f32),
                 pltpu.VMEM((3, ext, LANES), f32),
             ),
             in_specs=[in_hbm] * 5,
             out_specs=(in_vmem, in_vmem),
             scratch_shapes=[
                 pltpu.VMEM((3, 2, levels, rows, LANES), f32),
-                pltpu.VMEM((3, rows + 4, levels, columns), f32),
+                pltpu.VMEM((3, rows, levels, columns), f32),
                 pltpu.VMEM((3, rows + 2, levels, columns), f32),
+                pltpu.VMEM((2, 3, 2, levels, SUB, LANES), f32),
                 pltpu.VMEM((2, 2, ext, LANES), f32),
                 pltpu.VMEM((5, ext, LANES), f32),
                 pltpu.VMEM((2, rows, LANES), f32),
                 pltpu.VMEM((ext, LANES), f32),
                 pltpu.VMEM((ext, LANES), f32),
                 pltpu.SMEM((levels,), f32),
-                pltpu.SemaphoreType.DMA((2, 5)),
+                pltpu.SemaphoreType.DMA((2, 3)),
+                pltpu.SemaphoreType.DMA((2, 2)),
                 pltpu.SemaphoreType.DMA,
                 pltpu.SemaphoreType.DMA((3, levels)),
-                pltpu.SemaphoreType.DMA((12,)),
-                pltpu.SemaphoreType.DMA((12,)),
+                pltpu.SemaphoreType.DMA((22,)),
+                pltpu.SemaphoreType.DMA((22,)),
             ],
             compiler_params=pltpu.CompilerParams(
                 collective_id=0, has_side_effects=True, vmem_limit_bytes=VMEM_MAIN
@@ -482,8 +497,8 @@
             in_specs=[in_vmem] * 2,
             out_specs=(in_hbm, in_hbm),
             scratch_shapes=[
-                pltpu.VMEM((3, rows, levels, columns), f32),
-                pltpu.SemaphoreType.DMA((GROUPS, 3, levels)),
+                pltpu.VMEM((3, levels, rows, columns), f32),
+                pltpu.SemaphoreType.DMA((rows // SUB, 3)),
             ],
             compiler_params=pltpu.CompilerParams(vmem_limit_bytes=VMEM_END),
             cost_estimate=pl.CostEstimate(

time: 16 us -> 17.3 us (1.081)
  Pallas kernels: 15.2 us -> 16.5 us
    pallas_call x1, Pallas kernels: 13.1 us -> 15 us  [body(): pl.pallas_call(run, out_shape=(pltpu.VMEM((3, 2, levels, rows, LANES), f3...]
    pallas_call x1, Pallas kernels: 2.16 us -> 1.42 us  [body(): pl.pallas_call(end, out_shape=(jax.ShapeDtypeStruct(thickness.shape, f32)...]
where the time goes in v3:
time: 17.3 us; the launch traced here: 17.1 us
  Pallas kernels  16.5 us (95%)
  between operations  0.64 us (4%)
    pallas_call x1, Pallas kernels, body(): pl.pallas_call(run, out_shape=(pltpu.VMEM((3, 2, levels, rows, LANES), f3...  15 us
    pallas_call x1, Pallas kernels, body(): pl.pallas_call(end, out_shape=(jax.ShapeDtypeStruct(thickness.shape, f32)...  1.42 us

profile of v3, /device:TPU:1, one launch (start us, length us, event | category | flops | bytes accessed | tf_op | source)
XLA Modules:
  0.0 17.1 jit_solution(11792753286384422382)
XLA Ops:
  0.6 15.0 %shard_map.68 = (f32[3,2,8,64,128]{4,3,2,1,0:T(8,128)S(1)}, f32[3,80,128]{2,1,0:T(8,128)S(1)}) custom-call(f32[8,64,256]{2,1,0:T(8,128)} %refs_0_.1, f32[2,8,64,256]{3,2,1,0:T(8,128)} %refs_1_.1, f32[64,256]{1,0:T(8,128)} %refs_2_.1, f32[64,256]{1,0:T(8,128)} %refs_3_.1, f32[8]{0:T(128)} %refs_4_.1), custom_call_target="tpu_custom_call" | custom-call | flops 26214400 | bytes 3670016 | tf_op jit(solution)/shard_map/pallas_call | solution.py:454
  15.7 1.4 %shard_map.69 = (f32[8,64,256]{2,1,0:T(8,128)}, f32[2,8,64,256]{3,2,1,0:T(8,128)}) custom-call(f32[3,2,8,64,128]{4,3,2,1,0:T(8,128)S(1)} %get-tuple-element.4.refs_0_, f32[3,80,128]{2,1,0:T(8,128)S(1)} %get-tuple-element.5.refs_1_), custom_call_target="tpu_custom_call" | custom-call | flops 131072 | bytes 3145728 | tf_op jit(solution)/shard_map/pallas_call | solution.py:491

commit v4 on v3

--- a/solution.py
+++ b/solution.py
@@ -13,6 +13,11 @@
 VMEM_MAIN = 58 * 1024 * 1024
 VMEM_END = 16 * 1024 * 1024
 MESH = pl.DeviceIdType.MESH
+
+
+def quotient(top, below):
+    inverse = pl.reciprocal(below, approx=True)
+    return top * (inverse * (2.0 - below * inverse))
 
 
 def kernel(
@@ -183,6 +188,21 @@
         remote(5, pack.at[1, first], east_pack.at[ext_last], me_x - 1, south),
     ]
 
+    greeted = 2 + 3 * west_open.astype(jnp.int32) + 3 * east_open.astype(jnp.int32)
+    pl.semaphore_wait(barrier, greeted)
+    for copy in along_y:
+        copy.start()
+
+    @pl.when(east_open)
+    def _():
+        for copy in to_east:
+            copy.start()
+
+    @pl.when(west_open)
+    def _():
+        for copy in to_west:
+            copy.start()
+
     before_end = lane < LANES - 1
     at_start = lane == 0
 
@@ -214,7 +234,7 @@
             lambda e, v, un, u, f: (e - v) - (un - u) + f,
             eastward(along_y), along_y, along_x_n, along_x, coriolis,
         )
-        spin = each(lambda z, a, b: z / (a + b), vort, wide, wide_n)
+        spin = each(lambda z, a, b: quotient(z, a + b), vort, wide, wide_n)
         turn_y = each(lambda w, a, b: w * (a + b), spin, flux_y, eastward(flux_y))
         turn_x = each(lambda w, a, b: w * (a + b), spin, flux, flux_n)
         square = each(lambda a: a * a, along_x_n)
@@ -285,26 +305,7 @@
         carry, _ = advance(carry, start_row(start), fixed_row(0, start), fixed_row(1, start - 1))
         return carry
 
-    carry = first_begin(1)
-    early = 1 + UNROLL * ((rows - 2) // (2 * UNROLL))
-    carry = sweep(carry, 1, early, first_step)
-
-    greeted = 2 + 3 * west_open.astype(jnp.int32) + 3 * east_open.astype(jnp.int32)
-    pl.semaphore_wait(barrier, greeted)
-    for copy in along_y:
-        copy.start()
-
-    @pl.when(east_open)
-    def _():
-        for copy in to_east:
-            copy.start()
-
-    @pl.when(west_open)
-    def _():
-        for copy in to_west:
-            copy.start()
-
-    sweep(carry, early, rows - 1, first_step)
+    sweep(first_begin(1), 1, rows - 1, first_step)
 
     out_flat = [[result.at[item, half].reshape(levels * rows, LANES) for half in range(2)] for item in range(3)]
 
@@ -372,7 +373,7 @@
         flux = wide * along_x
         flux_y = (thick + north_of(thick)) * along_y
         vort = (turn(along_y, -1) - along_y) - (north_of(along_x) - along_x) + coriolis
-        spin = vort / (wide + north_of(wide))
+        spin = quotient(vort, wide + north_of(wide))
         turn_y = spin * (flux_y + turn(flux_y, -1))
         turn_x = spin * (flux + north_of(flux))
         square = along_x * along_x

time: 17.3 us -> 16.4 us (0.948)
  Pallas kernels: 16.5 us -> 15.6 us
    pallas_call x1, Pallas kernels: 15 us -> 14.2 us  [body(): pl.pallas_call(run, out_shape=(pltpu.VMEM((3, 2, levels, rows, LANES), f3...]
where the time goes in v4:
time: 16.4 us; the launch traced here: 16.3 us
  Pallas kernels  15.6 us (95%)
  between operations  0.64 us (4%)
    pallas_call x1, Pallas kernels, body(): pl.pallas_call(run, out_shape=(pltpu.VMEM((3, 2, levels, rows, LANES), f3...  14.2 us
    pallas_call x1, Pallas kernels, body(): pl.pallas_call(end, out_shape=(jax.ShapeDtypeStruct(thickness.shape, f32)...  1.42 us

profile of v4, /device:TPU:1, one launch (start us, length us, event | category | flops | bytes accessed | tf_op | source)
XLA Modules:
  0.0 16.3 jit_solution(15875525695537702993)
XLA Ops:
  0.6 14.2 %shard_map.68 = (f32[3,2,8,64,128]{4,3,2,1,0:T(8,128)S(1)}, f32[3,80,128]{2,1,0:T(8,128)S(1)}) custom-call(f32[8,64,256]{2,1,0:T(8,128)} %refs_0_.1, f32[2,8,64,256]{3,2,1,0:T(8,128)} %refs_1_.1, f32[64,256]{1,0:T(8,128)} %refs_2_.1, f32[64,256]{1,0:T(8,128)} %refs_3_.1, f32[8]{0:T(128)} %refs_4_.1), custom_call_target="tpu_custom_call" | custom-call | flops 26214400 | bytes 3670016 | tf_op jit(solution)/shard_map/pallas_call | solution.py:455
  14.8 1.4 %shard_map.69 = (f32[8,64,256]{2,1,0:T(8,128)}, f32[2,8,64,256]{3,2,1,0:T(8,128)}) custom-call(f32[3,2,8,64,128]{4,3,2,1,0:T(8,128)S(1)} %get-tuple-element.4.refs_0_, f32[3,80,128]{2,1,0:T(8,128)S(1)} %get-tuple-element.5.refs_1_), custom_call_target="tpu_custom_call" | custom-call | flops 131072 | bytes 3145728 | tf_op jit(solution)/shard_map/pallas_call | solution.py:492

commit v5 on v2

--- a/solution.py
+++ b/solution.py
@@ -10,10 +10,14 @@
 SUB = 8
 GROUP = 16
 UNROLL = 10
-GROUPS = 2
 VMEM_MAIN = 58 * 1024 * 1024
 VMEM_END = 16 * 1024 * 1024
 MESH = pl.DeviceIdType.MESH
+
+
+def quotient(top, below):
+    inverse = pl.reciprocal(below, approx=True)
+    return top * (inverse * (2.0 - below * inverse))
 
 
 def kernel(
@@ -145,8 +149,10 @@
 
     first = pl.ds(0, SUB)
     last = pl.ds(rows - SUB, SUB)
-    own_first = pl.ds(SUB, SUB)
-    own_last = pl.ds(rows, SUB)
+    own_first = pl.ds(SUB, 2)
+    own_last = pl.ds(rows + SUB - 2, 2)
+    ext_south = pl.ds(SUB - 2, 2)
+    ext_north = pl.ds(rows + SUB, 2)
     ext_last = pl.ds(rows + SUB, SUB)
     ext_own = pl.ds(SUB, rows)
 
@@ -163,10 +169,10 @@
     along_y = [
         remote(0, by_row.at[:, pl.ds(rows, 2)], by_row.at[:, pl.ds(0, 2)], me_x, north),
         remote(1, by_row.at[:, pl.ds(2, 2)], by_row.at[:, pl.ds(rows + 2, 2)], me_x, south),
-        remote(2, fixed.at[:, :, own_last], fixed.at[:, :, first], me_x, north),
-        remote(3, fixed.at[:, :, own_first], fixed.at[:, :, ext_last], me_x, south),
-        remote(4, strip.at[:, own_last], strip.at[:, first], me_x, north),
-        remote(5, strip.at[:, own_first], strip.at[:, ext_last], me_x, south),
+        remote(2, fixed.at[:, :, own_last], fixed.at[:, :, ext_south], me_x, north),
+        remote(3, fixed.at[:, :, own_first], fixed.at[:, :, ext_north], me_x, south),
+        remote(4, strip.at[:, own_last], strip.at[:, ext_south], me_x, north),
+        remote(5, strip.at[:, own_first], strip.at[:, ext_north], me_x, south),
     ]
     to_east = [
         remote(6, pack.at[0], west_pack.at[ext_own], me_x + 1, me_y),
@@ -225,7 +231,7 @@
             lambda e, v, un, u, f: (e - v) - (un - u) + f,
             eastward(along_y), along_y, along_x_n, along_x, coriolis,
         )
-        spin = each(lambda z, a, b: z / (a + b), vort, wide, wide_n)
+        spin = each(lambda z, a, b: quotient(z, a + b), vort, wide, wide_n)
         turn_y = each(lambda w, a, b: w * (a + b), spin, flux_y, eastward(flux_y))
         turn_x = each(lambda w, a, b: w * (a + b), spin, flux, flux_n)
         square = each(lambda a: a * a, along_x_n)
@@ -289,13 +295,15 @@
 
     first_sweep(1, rows - 1)
 
+    out_flat = [[result.at[item, half].reshape(levels * rows, LANES) for half in range(2)] for item in range(3)]
+
     def second_step(carry, row):
         after, rates = advance(carry, mid_row(row + 1), fixed_row(0, row + 1), fixed_row(1, row))
         start = start_row(row)
         for item in range(3):
             for half in range(2):
                 value = 0.5 * (start[item][half] + carry[item][half]) + 0.25 * time_step * rates[item][half]
-                result[item, row, :, pl.ds(half * LANES, LANES)] = value
+                out_flat[item][half][pl.ds(row, levels, stride=rows), :] = value
         return after
 
     def second_sweep(start, stop):
@@ -351,7 +359,7 @@
         flux = wide * along_x
         flux_y = (thick + north_of(thick)) * along_y
         vort = (turn(along_y, -1) - along_y) - (north_of(along_x) - along_x) + coriolis
-        spin = vort / (wide + north_of(wide))
+        spin = quotient(vort, wide + north_of(wide))
         turn_y = spin * (flux_y + turn(flux_y, -1))
         turn_x = spin * (flux + north_of(flux))
         square = along_x * along_x
@@ -393,33 +401,25 @@
 
 def finish(rows, result, strip_out, h_out, vel_out, merged, store_sem):
     levels = SUB
+    blocks = rows // SUB
     lane = lax.broadcasted_iota(jnp.int32, (SUB, LANES), 1)
-    size = rows // GROUPS
 
     stores = []
-    for group in range(GROUPS):
-
-        def merge(step, _):
-            row = group * size + step
-            for item in range(3):
-                value = jnp.broadcast_to(strip_out[item, pl.ds(row + SUB, 1), :], (SUB, LANES))
-                moved = pltpu.roll(value, SUB, 1, stride=GROUP, stride_axis=0)
-                low = result[item, row, :, pl.ds(0, LANES)]
-                high = result[item, row, :, pl.ds(LANES, LANES)]
-                merged[item, row, :, pl.ds(0, LANES)] = jnp.where(lane < 2, moved, low)
-                merged[item, row, :, pl.ds(LANES, LANES)] = jnp.where(lane >= LANES - 4, moved, high)
-            return 0
-
-        lax.fori_loop(0, size, merge, 0, unroll=SUB)
-        part = pl.ds(group * size, size)
+    for block in range(blocks):
+        part = pl.ds(block * SUB, SUB)
         for item in range(3):
+            value = strip_out[item, pl.ds(block * SUB + SUB, SUB), :]
             for lev in range(levels):
-                target = h_out.at[lev, part] if item == 0 else vel_out.at[item - 1, lev, part]
-                copy = pltpu.make_async_copy(
-                    merged.at[item, part, lev], target, store_sem.at[group, item, lev]
-                )
-                copy.start()
-                stores.append(copy)
+                moved = pltpu.roll(value, (SUB + GROUP * lev) % LANES, 1)
+                low = result[item, 0, lev, part, :]
+                high = result[item, 1, lev, part, :]
+                merged[item, lev, part, pl.ds(0, LANES)] = jnp.where(lane < 2, moved, low)
+                merged[item, lev, part, pl.ds(LANES, LANES)] = jnp.where(lane >= LANES - 4, moved, high)
+        targets = [h_out.at[:, part], vel_out.at[0, :, part], vel_out.at[1, :, part]]
+        for item in range(3):
+            copy = pltpu.make_async_copy(merged.at[item, :, part], targets[item], store_sem.at[block, item])
+            copy.start()
+            stores.append(copy)
     for copy in stores:
         copy.wait()
 
@@ -441,7 +441,7 @@
         result, strip_out = pl.pallas_call(
             run,
             out_shape=(
-                pltpu.VMEM((3, rows, levels, columns), f32),
+                pltpu.VMEM((3, 2, levels, rows, LANES), f32),
                 pltpu.VMEM((3, ext, LANES), f32),
             ),
             in_specs=[in_hbm] * 5,
@@ -482,8 +482,8 @@
             in_specs=[in_vmem] * 2,
             out_specs=(in_hbm, in_hbm),
             scratch_shapes=[
-                pltpu.VMEM((3, rows, levels, columns), f32),
-                pltpu.SemaphoreType.DMA((GROUPS, 3, levels)),
+                pltpu.VMEM((3, levels, rows, columns), f32),
+                pltpu.SemaphoreType.DMA((rows // SUB, 3)),
             ],
             compiler_params=pltpu.CompilerParams(vmem_limit_bytes=VMEM_END),
             cost_estimate=pl.CostEstimate(

time: 16 us -> 15.1 us (0.944)
  Pallas kernels: 15.2 us -> 14.3 us
    pallas_call x1, Pallas kernels: 2.16 us -> 1.42 us  [body(): pl.pallas_call(end, out_shape=(jax.ShapeDtypeStruct(thickness.shape, f32)...]
    pallas_call x1, Pallas kernels: 13.1 us -> 12.9 us  [body(): pl.pallas_call(run, out_shape=(pltpu.VMEM((3, 2, levels, rows, LANES), f3...]
where the time goes in v5:
time: 15.1 us; the launch traced here: 14.9 us
  Pallas kernels  14.3 us (95%)
  between operations  0.64 us (4%)
    pallas_call x1, Pallas kernels, body(): pl.pallas_call(run, out_shape=(pltpu.VMEM((3, 2, levels, rows, LANES), f3...  12.9 us
    pallas_call x1, Pallas kernels, body(): pl.pallas_call(end, out_shape=(jax.ShapeDtypeStruct(thickness.shape, f32)...  1.42 us

profile of v5, /device:TPU:1, one launch (start us, length us, event | category | flops | bytes accessed | tf_op | source)
XLA Modules:
  0.0 14.9 jit_solution(9468438336833141118)
XLA Ops:
  0.6 12.9 %shard_map.68 = (f32[3,2,8,64,128]{4,3,2,1,0:T(8,128)S(1)}, f32[3,80,128]{2,1,0:T(8,128)S(1)}) custom-call(f32[8,64,256]{2,1,0:T(8,128)} %refs_0_.1, f32[2,8,64,256]{3,2,1,0:T(8,128)} %refs_1_.1, f32[64,256]{1,0:T(8,128)} %refs_2_.1, f32[64,256]{1,0:T(8,128)} %refs_3_.1, f32[8]{0:T(128)} %refs_4_.1), custom_call_target="tpu_custom_call" | custom-call | flops 26214400 | bytes 3670016 | tf_op jit(solution)/shard_map/pallas_call | solution.py:441
  13.5 1.4 %shard_map.69 = (f32[8,64,256]{2,1,0:T(8,128)}, f32[2,8,64,256]{3,2,1,0:T(8,128)}) custom-call(f32[3,2,8,64,128]{4,3,2,1,0:T(8,128)S(1)} %get-tuple-element.4.refs_0_, f32[3,80,128]{2,1,0:T(8,128)S(1)} %get-tuple-element.5.refs_1_), custom_call_target="tpu_custom_call" | custom-call | flops 131072 | bytes 3145728 | tf_op jit(solution)/shard_map/pallas_call | solution.py:476

commit v6 on v5

--- a/solution.py
+++ b/solution.py
@@ -9,7 +9,7 @@
 LANES = 128
 SUB = 8
 GROUP = 16
-UNROLL = 10
+UNROLL = 20
 VMEM_MAIN = 58 * 1024 * 1024
 VMEM_END = 16 * 1024 * 1024
 MESH = pl.DeviceIdType.MESH

time: 15.1 us -> 17.6 us (1.17)
  Pallas kernels: 14.3 us -> 16.9 us
    pallas_call x1, Pallas kernels: 12.9 us -> 15.4 us  [body(): pl.pallas_call(run, out_shape=(pltpu.VMEM((3, 2, levels, rows, LANES), f3...]
where the time goes in v6:
time: 17.6 us; the launch traced here: 17.5 us
  Pallas kernels  16.9 us (96%)
  between operations  0.64 us (4%)
    pallas_call x1, Pallas kernels, body(): pl.pallas_call(run, out_shape=(pltpu.VMEM((3, 2, levels, rows, LANES), f3...  15.4 us
    pallas_call x1, Pallas kernels, body(): pl.pallas_call(end, out_shape=(jax.ShapeDtypeStruct(thickness.shape, f32)...  1.42 us

profile of v6, /device:TPU:1, one launch (start us, length us, event | category | flops | bytes accessed | tf_op | source)
XLA Modules:
  0.0 17.5 jit_solution(10873121514551366974)
XLA Ops:
  0.6 15.4 %shard_map.68 = (f32[3,2,8,64,128]{4,3,2,1,0:T(8,128)S(1)}, f32[3,80,128]{2,1,0:T(8,128)S(1)}) custom-call(f32[8,64,256]{2,1,0:T(8,128)} %refs_0_.1, f32[2,8,64,256]{3,2,1,0:T(8,128)} %refs_1_.1, f32[64,256]{1,0:T(8,128)} %refs_2_.1, f32[64,256]{1,0:T(8,128)} %refs_3_.1, f32[8]{0:T(128)} %refs_4_.1), custom_call_target="tpu_custom_call" | custom-call | flops 26214400 | bytes 3670016 | tf_op jit(solution)/shard_map/pallas_call | solution.py:441
  16.1 1.4 %shard_map.69 = (f32[8,64,256]{2,1,0:T(8,128)}, f32[2,8,64,256]{3,2,1,0:T(8,128)}) custom-call(f32[3,2,8,64,128]{4,3,2,1,0:T(8,128)S(1)} %get-tuple-element.4.refs_0_, f32[3,80,128]{2,1,0:T(8,128)S(1)} %get-tuple-element.5.refs_1_), custom_call_target="tpu_custom_call" | custom-call | flops 131072 | bytes 3145728 | tf_op jit(solution)/shard_map/pallas_call | solution.py:476

commit v7 on v6

--- a/solution.py
+++ b/solution.py
@@ -9,7 +9,7 @@
 LANES = 128
 SUB = 8
 GROUP = 16
-UNROLL = 20
+UNROLL = 6
 VMEM_MAIN = 58 * 1024 * 1024
 VMEM_END = 16 * 1024 * 1024
 MESH = pl.DeviceIdType.MESH
@@ -288,12 +288,12 @@
             carry = step(carry, row)
         return carry
 
-    def first_sweep(start, stop):
+    def first_begin(start):
         carry = begin(start_row(start - 1))
         carry, _ = advance(carry, start_row(start), fixed_row(0, start), fixed_row(1, start - 1))
-        sweep(carry, start, stop, first_step)
-
-    first_sweep(1, rows - 1)
+        return carry
+
+    sweep(first_begin(1), 1, rows - 1, first_step)
 
     out_flat = [[result.at[item, half].reshape(levels * rows, LANES) for half in range(2)] for item in range(3)]
 
@@ -306,12 +306,12 @@
                 out_flat[item][half][pl.ds(row, levels, stride=rows), :] = value
         return after
 
-    def second_sweep(start, stop):
+    def second_begin(start):
         carry = begin(mid_row(start - 1))
         carry, _ = advance(carry, mid_row(start), fixed_row(0, start), fixed_row(1, start - 1))
-        sweep(carry, start, stop, second_step)
-
-    second_sweep(2, rows - 2)
+        return carry
+
+    sweep(second_begin(2), 2, rows - 2, second_step)
 
     for copy in along_y:
         copy.wait_recv()
@@ -326,10 +326,23 @@
         for copy in to_west:
             copy.wait_recv()
 
-    first_sweep(-1, 1)
-    first_sweep(rows - 1, rows + 1)
-    second_sweep(0, 2)
-    second_sweep(rows - 2, rows)
+
+    def first_edge(side, _):
+        start = side * rows - 1
+        carry = first_begin(start)
+        for step in range(2):
+            carry = first_step(carry, start + step)
+        return 0
+
+    def second_edge(side, _):
+        start = side * (rows - 2)
+        carry = second_begin(start)
+        for step in range(2):
+            carry = second_step(carry, start + step)
+        return 0
+
+    lax.fori_loop(0, 2, first_edge, 0)
+    lax.fori_loop(0, 2, second_edge, 0)
 
     wide_lane = lax.broadcasted_iota(jnp.int32, (ext, LANES), 1)
     wide_place = wide_lane - (wide_lane // GROUP) * GROUP

time: 17.6 us -> 15.9 us (0.903)
  Pallas kernels: 16.9 us -> 15.1 us
    pallas_call x1, Pallas kernels: 15.4 us -> 13.7 us  [body(): pl.pallas_call(run, out_shape=(pltpu.VMEM((3, 2, levels, rows, LANES), f3...]
where the time goes in v7:
time: 15.9 us; the launch traced here: 15.7 us
  Pallas kernels  15.1 us (95%)
  between operations  0.64 us (4%)
    pallas_call x1, Pallas kernels, body(): pl.pallas_call(run, out_shape=(pltpu.VMEM((3, 2, levels, rows, LANES), f3...  13.7 us
    pallas_call x1, Pallas kernels, body(): pl.pallas_call(end, out_shape=(jax.ShapeDtypeStruct(thickness.shape, f32)...  1.42 us

profile of v7, /device:TPU:1, one launch (start us, length us, event | category | flops | bytes accessed | tf_op | source)
XLA Modules:
  0.0 15.7 jit_solution(7067746156622367023)
XLA Ops:
  0.6 13.7 %shard_map.68 = (f32[3,2,8,64,128]{4,3,2,1,0:T(8,128)S(1)}, f32[3,80,128]{2,1,0:T(8,128)S(1)}) custom-call(f32[8,64,256]{2,1,0:T(8,128)} %refs_0_.1, f32[2,8,64,256]{3,2,1,0:T(8,128)} %refs_1_.1, f32[64,256]{1,0:T(8,128)} %refs_2_.1, f32[64,256]{1,0:T(8,128)} %refs_3_.1, f32[8]{0:T(128)} %refs_4_.1), custom_call_target="tpu_custom_call" | custom-call | flops 26214400 | bytes 3670016 | tf_op jit(solution)/shard_map/pallas_call | solution.py:454
  14.3 1.4 %shard_map.69 = (f32[8,64,256]{2,1,0:T(8,128)}, f32[2,8,64,256]{3,2,1,0:T(8,128)}) custom-call(f32[3,2,8,64,128]{4,3,2,1,0:T(8,128)S(1)} %get-tuple-element.4.refs_0_, f32[3,80,128]{2,1,0:T(8,128)S(1)} %get-tuple-element.5.refs_1_), custom_call_target="tpu_custom_call" | custom-call | flops 131072 | bytes 3145728 | tf_op jit(solution)/shard_map/pallas_call | solution.py:489
